TPU v7x, 256 devices: a whole 4x4x8 slice. The times are simulated.
256 devices in a mesh: outer: 8 (over y, x_lo), inner: 32 (over x_hi, z, core).
Axes of the slice: x: 4 (x_hi: 2, x_lo: 2; x = x_hi * 2 + x_lo), y: 4, z: 8, core: 2. Of those that a mesh axis runs over, the one named last changes fastest.
Arguments:
- volume: bfloat16 [4, 128, 128, 1024], P(None, 'outer', 'inner'), may hold values from -6 to 6
- cotangent: bfloat16 [4, 128, 128, 1024], P(None, 'outer', 'inner'), may hold values from -6 to 6
- gain_width: bfloat16 [1024], replicated, may hold values from 0.25 to 1.75
- qkv_width: bfloat16 [1024, 1536], replicated, may hold values from -5 to 5
- out_width: bfloat16 [512, 1024], replicated, may hold values from -0.25 to 0.25
- gain_height: bfloat16 [1024], replicated, may hold values from 0.25 to 1.75
- qkv_height: bfloat16 [1024, 1536], replicated, may hold values from -5 to 5
- out_height: bfloat16 [512, 1024], replicated, may hold values from -0.25 to 0.25
Outputs:
- result: bfloat16 [4, 128, 128, 1024], P(None, 'outer', 'inner')
- volume_grad: bfloat16 [4, 128, 128, 1024], P(None, 'outer', 'inner')
All inputs are finite; a program needn't handle non-finite values.
Results may differ from a plain program's by a relative error of at most 0.015.
Values may be sent and summed in bfloat16 or wider, within the bound.
A program may use at most 64 MiB of HBM per device.

v0:
```python
import jax
import jax.numpy as jnp
from jax import lax
from jax.sharding import PartitionSpec as P

HEADS = 8


def sublayer(rows, gain, qkv, out):
    lines, length, width = rows.shape
    inner = out.shape[0]
    heads = HEADS
    hdim = inner // heads
    values32 = rows.astype(jnp.float32)
    meansq = jnp.mean(values32 * values32, axis=-1, keepdims=True)
    normed = (values32 * lax.rsqrt(meansq + 1e-06) * gain.astype(jnp.float32)).astype(jnp.bfloat16)
    proj = jnp.dot(
        normed.reshape(lines * length, width), qkv, preferred_element_type=jnp.float32
    ).astype(jnp.bfloat16)
    proj = proj.reshape(lines, length, 3, heads, hdim)
    query = proj[:, :, 0]
    keys = proj[:, :, 1]
    vals = proj[:, :, 2]
    scores = jnp.einsum("rqhd,rkhd->rhqk", query, keys, preferred_element_type=jnp.float32) * 0.125
    top = jnp.max(scores, axis=-1, keepdims=True)
    expo = jnp.exp(scores - top)
    probs = (expo / jnp.sum(expo, axis=-1, keepdims=True)).astype(jnp.bfloat16)
    mixed = jnp.einsum("rhqk,rkhd->rqhd", probs, vals, preferred_element_type=jnp.float32).astype(
        jnp.bfloat16
    )
    mixed = mixed.reshape(lines * length, inner)
    branch = jnp.dot(mixed, out, preferred_element_type=jnp.float32).reshape(lines, length, width)
    return (values32 + branch).astype(jnp.bfloat16)


def to_width(block):
    frames, rows_h, cols_w, width = block.shape
    return lax.all_to_all(
        block.reshape(frames * rows_h, cols_w, width),
        "inner",
        split_axis=0,
        concat_axis=1,
        tiled=True,
    )


def from_width(lines, shape):
    return lax.all_to_all(lines, "inner", split_axis=1, concat_axis=0, tiled=True).reshape(shape)


def to_height(block):
    frames, rows_h, cols_w, width = block.shape
    turned = block.transpose(0, 2, 1, 3).reshape(frames * cols_w, rows_h, width)
    return lax.all_to_all(turned, "outer", split_axis=0, concat_axis=1, tiled=True)


def from_height(lines, shape):
    frames, rows_h, cols_w, width = shape
    back = lax.all_to_all(lines, "outer", split_axis=1, concat_axis=0, tiled=True)
    return back.reshape(frames, cols_w, rows_h, width).transpose(0, 2, 1, 3)


def on_device(
    volume, cotangent, gain_width, qkv_width, out_width, gain_height, qkv_height, out_height
):
    shape = volume.shape

    def width_layer(rows):
        return sublayer(rows, gain_width, qkv_width, out_width)

    def height_layer(rows):
        return sublayer(rows, gain_height, qkv_height, out_height)

    lines_w = to_width(volume)
    done_w, pull_w = jax.vjp(width_layer, lines_w)
    middle = from_width(done_w, shape)
    lines_h = to_height(middle)
    done_h, pull_h = jax.vjp(height_layer, lines_h)
    result = from_height(done_h, shape)
    middle_grad = from_height(pull_h(to_height(cotangent))[0], shape)
    volume_grad = from_width(pull_w(to_width(middle_grad))[0], shape)
    return (result, volume_grad)


def solution(mesh):
    in_specs = (
        P(None, "outer", "inner", None),
        P(None, "outer", "inner", None),
        P(),
        P(),
        P(),
        P(),
        P(),
        P(),
    )
    out_specs = (P(None, "outer", "inner", None), P(None, "outer", "inner", None))
    return jax.shard_map(
        on_device, mesh=mesh, in_specs=in_specs, out_specs=out_specs, check_vma=False
    )
```

profile of v0, /device:TPU:1, one launch (start us, length us, event | category | flops | bytes accessed | tf_op | source)
XLA Modules:
  0.0 251.3 jit_solution(2977962879948149952)
XLA Ops:
  0.6 12.9 %all-to-all-start = ((bf16[64,4,1024]{2,1,0:T(4,128)(2,1)}), bf16[64,4,1024]{2,1,0:T(4,128)(2,1)}, u32[]{:S(2)}, u32[]{:S(2)}) async-start(bf16[64,4,1024]{2,1,0:T(4,128)(2,1)} %bitcast.208), calls=%async_computation | async-start | bytes 1048576 | tf_op jit(solution)/shard_map/all_to_all | solution.py:38
  14.3 17.4 %all-to-all-done = bf16[64,4,1024]{2,1,0:T(4,128)(2,1)} async-done(((bf16[64,4,1024]{2,1,0:T(4,128)(2,1)}), bf16[64,4,1024]{2,1,0:T(4,128)(2,1)}, u32[]{:S(2)}, u32[]{:S(2)}) %all-to-all-start) | async-done | bytes 524320 | tf_op jit(solution)/shard_map/all_to_all | solution.py:38
  33.9 2.6 %reshape.223 = f32[256,1024]{1,0:T(8,128)} reshape(f32[2,32,4,1024]{3,2,1,0:T(4,128)} %copy.279) | data formatting | bytes 2097152 | tf_op jit(solution)/shard_map/jvp()/convert_element_type | solution.py:14
  36.5 2.6 %reshape.222 = f32[2,128,1024]{2,1,0:T(8,128)} reshape(f32[2,32,4,1024]{3,2,1,0:T(4,128)} %copy.279) | data formatting | bytes 2097152 | tf_op jit(solution)/shard_map/jvp()/convert_element_type | solution.py:14
  40.8 4.1 %convolution_convert_fusion.1 = bf16[256,1536]{1,0:T(8,128)(2,1)} fusion(bf16[1024,1536]{1,0:T(8,128)(2,1)} %param.11, f32[256,1024]{1,0:T(8,128)} %reshape.223, f32[1024]{0:T(1024)S(1)} %convert_element_type.215, f32[256]{0:T(256)S(1)} %rsqrt.33), kind=kOutput, calls=%fused_computation.1 | convolution fusion | flops 806486016 | bytes 4985856 | tf_op jit(solution)/shard_map/jvp()/dot_general | solution.py:17
  44.9 3.1 %reshape.240 = bf16[2,128,3,8,64]{4,3,2,1,0:T(8,128)(2,1)} reshape(bf16[256,1536]{1,0:T(8,128)(2,1)} %convolution_convert_fusion.1) | data formatting | bytes 1572864 | tf_op jit(solution)/shard_map/jvp()/reshape | solution.py:20
  48.0 2.5 %fusion.83 = (bf16[2,128,1,8,64]{4,3,2,1,0:T(8,128)(2,1)}, bf16[2,128,1,8,64]{4,3,2,1,0:T(8,128)(2,1)}, bf16[2,128,1,8,64]{4,3,2,1,0:T(8,128)(2,1)}) fusion(bf16[2,128,3,8,64]{4,3,2,1,0:T(8,128)(2,1)} %reshape.240), kind=kLoop, calls=%fused_computation.137 | loop fusion | bytes 1572864 | tf_op jit(solution)/shard_map/jvp()/slice | solution.py:23
  51.9 2.1 copy.354
  60.0 2.0 fusion
  63.3 6.5 %all-to-all-start.1 = ((bf16[2,128,1024]{2,0,1:T(2,128)(2,1)}), bf16[2,128,1024]{2,0,1:T(2,128)(2,1)}, u32[]{:S(2)}, u32[]{:S(2)}) async-start(bf16[2,128,1024]{2,0,1:T(2,128)(2,1)} %copy.289), calls=%async_computation.1 | async-start | bytes 1048576 | tf_op jit(solution)/shard_map/all_to_all | solution.py:48
  69.8 2.0 copy.304
  71.8 16.3 %all-to-all-done.1 = bf16[2,128,1024]{2,0,1:T(2,128)(2,1)} async-done(((bf16[2,128,1024]{2,0,1:T(2,128)(2,1)}), bf16[2,128,1024]{2,0,1:T(2,128)(2,1)}, u32[]{:S(2)}, u32[]{:S(2)}) %all-to-all-start.1) | async-done | bytes 524320 | tf_op jit(solution)/shard_map/all_to_all | solution.py:48
  88.1 4.2 %all-to-all-start.4 = ((bf16[16,16,1024]{2,1,0:T(8,128)(2,1)}), bf16[16,16,1024]{2,1,0:T(8,128)(2,1)}, u32[]{:S(2)}, u32[]{:S(2)}) async-start(bf16[16,16,1024]{2,1,0:T(8,128)(2,1)} %bitcast.197), calls=%async_computation.4 | async-start | bytes 1048576 | tf_op jit(solution)/shard_map/all_to_all | solution.py:54
  94.5 5.5 %all-to-all-done.4 = bf16[16,16,1024]{2,1,0:T(8,128)(2,1)} async-done(((bf16[16,16,1024]{2,1,0:T(8,128)(2,1)}), bf16[16,16,1024]{2,1,0:T(8,128)(2,1)}, u32[]{:S(2)}, u32[]{:S(2)}) %all-to-all-start.4) | async-done | bytes 524320 | tf_op jit(solution)/shard_map/all_to_all | solution.py:54
  100.0 4.3 %all-to-all-start.2 = ((bf16[16,16,1024]{2,1,0:T(8,128)(2,1)}), bf16[16,16,1024]{2,1,0:T(8,128)(2,1)}, u32[]{:S(2)}, u32[]{:S(2)}) async-start(bf16[16,16,1024]{2,1,0:T(8,128)(2,1)} %bitcast.196), calls=%async_computation.2 | async-start | bytes 1048576 | tf_op jit(solution)/shard_map/all_to_all | solution.py:54
  105.5 2.1 copy.305
  107.6 2.4 convolution_convert_fusion.13
  110.0 1.8 copy.307
  111.8 1.7 reshape.214
  118.5 1.9 convolution_convert_fusion
  120.4 3.1 %reshape.241 = bf16[2,128,3,8,64]{4,3,2,1,0:T(8,128)(2,1)} reshape(bf16[256,1536]{1,0:T(8,128)(2,1)} %convolution_convert_fusion) | data formatting | bytes 1572864 | tf_op jit(solution)/shard_map/jvp()/reshape | solution.py:20
  123.5 2.5 %fusion.82 = (bf16[2,128,1,8,64]{4,3,2,1,0:T(8,128)(2,1)}, bf16[2,128,1,8,64]{4,3,2,1,0:T(8,128)(2,1)}, bf16[2,128,1,8,64]{4,3,2,1,0:T(8,128)(2,1)}) fusion(bf16[2,128,3,8,64]{4,3,2,1,0:T(8,128)(2,1)} %reshape.241), kind=kLoop, calls=%fused_computation.136 | loop fusion | bytes 1572864 | tf_op jit(solution)/shard_map/jvp()/slice | solution.py:23
  126.0 2.0 copy.356
  128.0 2.0 copy.357
  132.6 2.0 copy.355
  134.7 1.9 fusion.13
  136.6 1.9 fusion.81
  145.4 2.1 fusion.18
  148.1 12.2 %all_to_all.108 = bf16[2,128,1024]{2,0,1:T(2,128)(2,1)S(1)} all-to-all(bf16[2,128,1024]{2,0,1:T(2,128)(2,1)S(1)} %copy.316), channel_id=1, replica_groups=mesh['outer'=8,'inner'=32] {'outer'}, dimensions={1} | all-to-all | bytes 1048576 | tf_op jit(solution)/shard_map/all_to_all | solution.py:59
  161.7 9.9 %all-to-all-start.6 = ((bf16[64,4,1024]{2,1,0:T(4,128)(2,1)}), bf16[64,4,1024]{2,1,0:T(4,128)(2,1)}, u32[]{:S(2)}, u32[]{:S(2)}) async-start(bf16[64,4,1024]{2,1,0:T(4,128)(2,1)} %copy.320), calls=%async_computation.6 | async-start | bytes 1048576 | tf_op jit(solution)/shard_map/all_to_all | solution.py:38
  173.3 2.0 fusion.1
  176.6 13.2 %all-to-all-done.6 = bf16[64,4,1024]{2,1,0:T(4,128)(2,1)} async-done(((bf16[64,4,1024]{2,1,0:T(4,128)(2,1)}), bf16[64,4,1024]{2,1,0:T(4,128)(2,1)}, u32[]{:S(2)}, u32[]{:S(2)}) %all-to-all-start.6) | async-done | bytes 524320 | tf_op jit(solution)/shard_map/all_to_all | solution.py:38
  189.8 4.4 %all-to-all-start.3 = ((bf16[2,128,1024]{2,0,1:T(2,128)(2,1)}), bf16[2,128,1024]{2,0,1:T(2,128)(2,1)}, u32[]{:S(2)}, u32[]{:S(2)}) async-start(bf16[2,128,1024]{2,0,1:T(2,128)(2,1)} %copy.301), calls=%async_computation.3 | async-start | bytes 1048576 | tf_op jit(solution)/shard_map/all_to_all | solution.py:59
  194.2 2.4 copy_bitcast_fusion
  197.7 2.0 reshape.218
  199.7 2.6 %convolution_convert_fusion.9 = bf16[256,512]{1,0:T(8,128)(2,1)} fusion(bf16[256,1024]{1,0:T(8,128)(2,1)} %reshape.218, bf16[512,1024]{1,0:T(8,128)(2,1)} %param.12), kind=kOutput, calls=%fused_computation.23 | convolution fusion | flops 268566528 | bytes 1835008 | tf_op jit(solution)/shard_map/transpose(jvp())/dot_general | solution.py:32
  202.3 1.8 copy.324
  204.1 1.7 reshape.219
  205.8 1.7 fusion.5
  207.5 1.8 fusion.17
  212.7 2.0 fusion.2
  214.7 2.5 reshape.231
  217.2 1.8 fusion.25
  219.1 2.0 copy.322
  221.2 2.1 fusion.19
  224.6 6.3 %all-to-all-start.7 = ((bf16[2,128,1024]{2,0,1:T(2,128)(2,1)}), bf16[2,128,1024]{2,0,1:T(2,128)(2,1)}, u32[]{:S(2)}, u32[]{:S(2)}) async-start(bf16[2,128,1024]{2,0,1:T(2,128)(2,1)} %copy.335), calls=%async_computation.7 | async-start | bytes 1048576 | tf_op jit(solution)/shard_map/all_to_all | solution.py:48
  233.4 15.9 %all-to-all-done.7 = bf16[2,128,1024]{2,0,1:T(2,128)(2,1)} async-done(((bf16[2,128,1024]{2,0,1:T(2,128)(2,1)}), bf16[2,128,1024]{2,0,1:T(2,128)(2,1)}, u32[]{:S(2)}, u32[]{:S(2)}) %all-to-all-start.7) | async-done | bytes 524320 | tf_op jit(solution)/shard_map/all_to_all | solution.py:48
  249.2 2.1 copy.336
  (98 shorter events, 44.2 us)
Async XLA Ops:
  0.6 117.9 %copy-start = (bf16[1024,1536]{1,0:T(8,128)(2,1)S(1)}, bf16[1024,1536]{1,0:T(8,128)(2,1)}, u32[]{:S(2)}) copy-start(bf16[1024,1536]{1,0:T(8,128)(2,1)} %param.14) | copy-start | bytes 9437188
  0.6 31.0 %all-to-all-start = ((bf16[64,4,1024]{2,1,0:T(4,128)(2,1)}), bf16[64,4,1024]{2,1,0:T(4,128)(2,1)}, u32[]{:S(2)}, u32[]{:S(2)}) async-start(bf16[64,4,1024]{2,1,0:T(4,128)(2,1)} %bitcast.208), calls=%async_computation | async-start | bytes 1048576 | tf_op jit(solution)/shard_map/all_to_all | solution.py:38
  51.9 5.4 %copy-start.8 = (bf16[2,128,1,8,64]{1,4,3,0,2:T(8,128)(2,1)}, bf16[2,128,1,8,64]{1,4,3,0,2:T(8,128)(2,1)S(1)}, u32[]{:S(2)}) copy-start(bf16[2,128,1,8,64]{1,4,3,0,2:T(8,128)(2,1)S(1)} %copy.353) | copy-start | bytes 786436
  55.3 1.0 copy-start.1
  63.3 41.1 %copy-start.13 = (bf16[1024]{0:T(1024)(128)(2,1)S(1)}, bf16[1024]{0:T(1024)(128)(2,1)}, u32[]{:S(2)}) copy-start(bf16[1024]{0:T(1024)(128)(2,1)} %param.13) | copy-start | bytes 6148
  63.3 24.8 %all-to-all-start.1 = ((bf16[2,128,1024]{2,0,1:T(2,128)(2,1)}), bf16[2,128,1024]{2,0,1:T(2,128)(2,1)}, u32[]{:S(2)}, u32[]{:S(2)}) async-start(bf16[2,128,1024]{2,0,1:T(2,128)(2,1)} %copy.289), calls=%async_computation.1 | async-start | bytes 1048576 | tf_op jit(solution)/shard_map/all_to_all | solution.py:48
  88.1 12.0 %all-to-all-start.4 = ((bf16[16,16,1024]{2,1,0:T(8,128)(2,1)}), bf16[16,16,1024]{2,1,0:T(8,128)(2,1)}, u32[]{:S(2)}, u32[]{:S(2)}) async-start(bf16[16,16,1024]{2,1,0:T(8,128)(2,1)} %bitcast.197), calls=%async_computation.4 | async-start | bytes 1048576 | tf_op jit(solution)/shard_map/all_to_all | solution.py:54
  100.0 13.5 %all-to-all-start.2 = ((bf16[16,16,1024]{2,1,0:T(8,128)(2,1)}), bf16[16,16,1024]{2,1,0:T(8,128)(2,1)}, u32[]{:S(2)}, u32[]{:S(2)}) async-start(bf16[16,16,1024]{2,1,0:T(8,128)(2,1)} %bitcast.196), calls=%async_computation.2 | async-start | bytes 1048576 | tf_op jit(solution)/shard_map/all_to_all | solution.py:54
  131.5 1.0 copy-start.3
  134.7 3.9 %copy-start.4 = (f32[2,8,128,128]{2,3,1,0:T(8,128)S(1)}, f32[2,8,128,128]{2,3,1,0:T(8,128)}, u32[]{:S(2)}) copy-start(f32[2,8,128,128]{2,3,1,0:T(8,128)} %copy-done.3) | copy-start | bytes 3145732
  134.7 3.9 %copy-start.11 = (bf16[2,128,1,8,64]{1,4,3,0,2:T(8,128)(2,1)S(1)}, bf16[2,128,1,8,64]{1,4,3,0,2:T(8,128)(2,1)}, u32[]{:S(2)}) copy-start(bf16[2,128,1,8,64]{1,4,3,0,2:T(8,128)(2,1)} %copy.356) | copy-start | bytes 786436
  138.5 1.7 copy-start.5
  138.5 1.1 copy-start.12
  139.6 0.9 copy-start.7
  143.0 1.0 copy-start.6
  161.7 28.0 %all-to-all-start.6 = ((bf16[64,4,1024]{2,1,0:T(4,128)(2,1)}), bf16[64,4,1024]{2,1,0:T(4,128)(2,1)}, u32[]{:S(2)}, u32[]{:S(2)}) async-start(bf16[64,4,1024]{2,1,0:T(4,128)(2,1)} %copy.320), calls=%async_computation.6 | async-start | bytes 1048576 | tf_op jit(solution)/shard_map/all_to_all | solution.py:38
  189.8 34.9 %all-to-all-start.3 = ((bf16[2,128,1024]{2,0,1:T(2,128)(2,1)}), bf16[2,128,1024]{2,0,1:T(2,128)(2,1)}, u32[]{:S(2)}, u32[]{:S(2)}) async-start(bf16[2,128,1024]{2,0,1:T(2,128)(2,1)} %copy.301), calls=%async_computation.3 | async-start | bytes 1048576 | tf_op jit(solution)/shard_map/all_to_all | solution.py:59
  205.8 3.5 %copy-start.2 = (f32[2,8,128,128]{2,3,1,0:T(8,128)S(1)}, f32[2,8,128,128]{2,3,1,0:T(8,128)}, u32[]{:S(2)}) copy-start(f32[2,8,128,128]{2,3,1,0:T(8,128)} %copy-done.1) | copy-start | bytes 3145732
  205.8 4.1 %copy-start.9 = (bf16[2,128,1,8,64]{1,4,3,0,2:T(8,128)(2,1)S(1)}, bf16[2,128,1,8,64]{1,4,3,0,2:T(8,128)(2,1)}, u32[]{:S(2)}) copy-start(bf16[2,128,1,8,64]{1,4,3,0,2:T(8,128)(2,1)} %copy-done.8) | copy-start | bytes 786436
  209.8 1.0 copy-start.10
  210.8 1.9 copy-start.14
  224.6 24.6 %all-to-all-start.7 = ((bf16[2,128,1024]{2,0,1:T(2,128)(2,1)}), bf16[2,128,1024]{2,0,1:T(2,128)(2,1)}, u32[]{:S(2)}, u32[]{:S(2)}) async-start(bf16[2,128,1024]{2,0,1:T(2,128)(2,1)} %copy.335), calls=%async_computation.7 | async-start | bytes 1048576 | tf_op jit(solution)/shard_map/all_to_all | solution.py:48
where the time goes:
time: 255 us; the launch traced here: 251 us
  local copies, waits for them, and re-layouts  68.9 us (27%)
  waiting for transfers between devices  68.2 us (27%)
  starting transfers between devices  48.5 us (19%)
  matrix products  31.7 us (12%)
  other arithmetic  20.6 us (8%)
  blocking collectives  12.2 us (5%)
    all_to_all x2, waiting for transfers between devices, from_width(): lax.all_to_all(lines, 'inner', split_axis=1, concat_axis=0, tiled=True)  32.1 us
    all_to_all x2, waiting for transfers between devices, to_width(): lax.all_to_all(block.reshape(frames * rows_h, cols_w, width), 'inner', sp...  30.6 us
    all_to_all x2, starting transfers between devices, to_width(): lax.all_to_all(block.reshape(frames * rows_h, cols_w, width), 'inner', sp...  22.8 us
    unnamed x38, local copies, waits for them, and re-layouts  18.4 us
    all_to_all x2, starting transfers between devices, from_width(): lax.all_to_all(lines, 'inner', split_axis=1, concat_axis=0, tiled=True)  12.8 us
    all_to_all x1, blocking collectives, from_height(): lax.all_to_all(lines, 'outer', split_axis=1, concat_axis=0, tiled=True)  12.2 us
    convert_element_type x6, local copies, waits for them, and re-layouts, sublayer(): values32 = rows.astype(jnp.float32)  9.22 us
    dot_general x4, matrix products, sublayer(): jnp.dot(normed.reshape(lines * length, width), qkv, preferred_element_typ...  9.09 us
  transfers between devices with their start and end apart: 7, of which 5 were waited for; matrix products, arithmetic and copies ran while one was open for 20% of the time, Pallas kernels for 0%

commit v1 on v0

v1 whole, which is shorter than its diff:
```python
import jax
import jax.numpy as jnp
from jax import lax
from jax.experimental import pallas as pl
from jax.experimental.pallas import tpu as pltpu
from jax.sharding import PartitionSpec as P

MESH = pl.DeviceIdType.MESH
BF = jnp.bfloat16
F32 = jnp.float32
D = 1024
INNER = 512
NI = 32
NO = 8
TOK = 256
PAIRS = 4
EPS = 1e-06


def dot(a, b):
    return jnp.dot(a, b, preferred_element_type=F32)


def dot_nt(a, b):
    return lax.dot_general(a, b, (((1,), (1,)), ((), ())), preferred_element_type=F32)


def dot_tn(a, b):
    return lax.dot_general(a, b, (((0,), (0,)), ((), ())), preferred_element_type=F32)


def home_to_height(r):
    return (r // 64) * 64 + (r % 16) * 4 + (r // 16) % 4


def arrive_to_lines(r):
    return ((r // 4) % 32) * 8 + (r // 128) * 4 + r % 4


def lines_to_pack(r):
    return ((r // 2) % 2) * 128 + (r // 8) * 4 + ((r // 4) % 2) * 2 + r % 2


def pack_to_height(r):
    return (r % 128) * 2 + r // 128


def one_hot(order, inverse):
    row = lax.broadcasted_iota(jnp.int32, (TOK, TOK), 0)
    col = lax.broadcasted_iota(jnp.int32, (TOK, TOK), 1)
    hit = (row == order(col)) if inverse else (col == order(row))
    return jnp.where(hit, 1.0, 0.0).astype(BF)


def low_rows(shape):
    return lax.broadcasted_iota(jnp.int32, shape, 0) % 8 < 4


def pack_wide(rows):
    g = rows.reshape(NI, 8, D)
    return jnp.concatenate([g[:, :, : D // 2], g[:, :, D // 2 :]], axis=1).reshape(2 * TOK, D // 2).astype(BF)


def unpack_wide(buf):
    g = buf.astype(F32).reshape(NI, 16, D // 2)
    return jnp.concatenate([g[:, :8], g[:, 8:]], axis=2).reshape(TOK, D)


def pack_narrow(rows):
    m = [rows[:, 128 * q : 128 * q + 128] for q in range(4)]
    low = low_rows((TOK, 128))
    parts = [
        jnp.where(low, m[0], pltpu.roll(m[1], 4, 0)),
        jnp.where(low, m[2], pltpu.roll(m[3], 4, 0)),
        jnp.where(low, pltpu.roll(m[0], TOK - 4, 0), m[1]),
        jnp.where(low, pltpu.roll(m[2], TOK - 4, 0), m[3]),
    ]
    return jnp.stack([p.reshape(32, 8, 128) for p in parts], axis=1).reshape(1024, 128).astype(BF)


def unpack_narrow(buf):
    g = buf.astype(F32).reshape(32, 4, 8, 128)
    v = [g[:, q].reshape(TOK, 128) for q in range(4)]
    low = low_rows((TOK, 128))
    return jnp.concatenate(
        [
            jnp.where(low, v[0], pltpu.roll(v[2], 4, 0)),
            jnp.where(low, pltpu.roll(v[0], TOK - 4, 0), v[2]),
            jnp.where(low, v[1], pltpu.roll(v[3], 4, 0)),
            jnp.where(low, pltpu.roll(v[1], TOK - 4, 0), v[3]),
        ],
        axis=1,
    )


def scale_of(v):
    return lax.rsqrt(jnp.mean(v * v, axis=-1, keepdims=True) + EPS)


def norm_back(v, dn, gain, resid):
    r = scale_of(v)
    gd = dn * gain
    c = jnp.sum(gd * v, axis=-1, keepdims=True) * (1.0 / D)
    return r * gd - v * (r * r * r * c) + resid


def lane_low():
    return lax.broadcasted_iota(jnp.int32, (128, 128), 1) < 64


def two_heads(a):
    low = lane_low()
    zero = jnp.zeros_like(a)
    return jnp.concatenate([jnp.where(low, a, zero), jnp.where(low, zero, a)], axis=0)


def one_pair(a):
    return jnp.where(lane_low(), a[:128], a[128:])


def unit_slices(line, pair):
    rows = pl.ds(line * 128, 128)
    return rows, [pl.ds(INNER * part + 128 * pair, 128) for part in range(3)]


def attend(proj, probs, mixed):
    for line in range(2):
        for pair in range(PAIRS):
            rows, (qs, ks, vs) = unit_slices(line, pair)
            s = dot_nt(two_heads(proj[rows, qs]), proj[rows, ks]) * 0.125
            e = jnp.exp(s - jnp.max(s, axis=-1, keepdims=True))
            p = e / jnp.sum(e, axis=-1, keepdims=True)
            probs[line * PAIRS + pair] = p
            mixed[rows, pl.ds(128 * pair, 128)] = one_pair(dot(p.astype(BF), proj[rows, vs])).astype(BF)


def attend_back(proj, probs, dmixed, dproj):
    for line in range(2):
        for pair in range(PAIRS):
            rows, (qs, ks, vs) = unit_slices(line, pair)
            p = probs[line * PAIRS + pair]
            do = two_heads(dmixed[rows, pl.ds(128 * pair, 128)])
            dp = dot_nt(do, proj[rows, vs]).astype(BF).astype(F32)
            dproj[rows, vs] = dot_tn(p.astype(BF), do).astype(BF)
            ds = p * (dp - jnp.sum(dp * p, axis=-1, keepdims=True)) * 0.125
            ds = ds.astype(BF)
            dproj[rows, qs] = one_pair(dot(ds, proj[rows, ks])).astype(BF)
            dproj[rows, ks] = dot_tn(ds, two_heads(proj[rows, qs])).astype(BF)


def far_first(k):
    return (4 + (1 - 2 * (k % 2)) * ((k + 1) // 2)) % 8


def kernel(
    vol_ref, cot_ref, gw_ref, gh_ref, qkvw_hbm, outw_hbm, qkvh_hbm, outh_hbm,
    res_ref, grad_ref,
    qkvw, outw, qkvh, outh, perms,
    s1, r1, s2, r2, s3, r3, s4, r4,
    sx, rx, sc, rc, sres, rres, smg, rmg,
    proj, projh, probs, probsh, mixed, mixedh, dproj, dmix, dmixh, mid,
    load_sem, send_sem, recv_sem, local_sem,
):
    i = lax.axis_index("inner")
    o = lax.axis_index("outer")
    ix, iz, ic = i // 16, (i // 2) % 8, i % 2
    oy, ol = o // 2, o % 2
    frame_w = ix * 2 + iz % 2
    slot_w = (iz // 2) * 2 + ic
    frame_h = (oy + iz) % 4
    same = frame_w == frame_h

    def device_of(f, j):
        return (f // 2) * 16 + ((j // 2) * 2 + f % 2) * 2 + j % 2

    def block_of(d):
        return (((d // 16) * 2 + (d // 2) % 2) * 8) + ((d // 4) % 4) * 2 + d % 2

    loads = [
        pltpu.make_async_copy(a, b, load_sem.at[n])
        for n, (a, b) in enumerate(((qkvw_hbm, qkvw), (outh_hbm, outh), (outw_hbm, outw), (qkvh_hbm, qkvh)))
    ]
    for load in loads:
        load.start()

    barrier = pltpu.get_barrier_semaphore()

    def greet_inner(k, c):
        pl.semaphore_signal(barrier, inc=1, device_id={"inner": (i + k) % NI}, device_id_type=MESH)
        return c

    def greet_outer(k, c):
        pl.semaphore_signal(barrier, inc=1, device_id={"outer": (o + k) % NO}, device_id_type=MESH)
        return c

    lax.fori_loop(1, NI, greet_inner, 0)
    lax.fori_loop(1, NO, greet_outer, 0)

    def rows16(b, n=1):
        return pl.ds(pl.multiple_of(b * 16, 16), 16 * n)

    def remote(src, dst, phase, target):
        return pltpu.make_async_remote_copy(
            src_ref=src, dst_ref=dst, send_sem=send_sem.at[phase], recv_sem=recv_sem.at[phase],
            device_id=target, device_id_type=MESH,
        )

    def all_inner(src, dst, phase, src_block, my_block):
        def go(k, c):
            dz = far_first(k // 2 % 8)
            dx = 1 - k // 16
            dc = 1 - k % 2
            d = ((ix + dx) % 2) * 16 + ((iz + dz) % 8) * 2 + (ic + dc) % 2
            remote(src.at[rows16(src_block(d))], dst.at[rows16(my_block)], phase, {"inner": d}).start()
            return c

        lax.fori_loop(0, NI - 1, go, 0)
        dst[rows16(my_block)] = src[rows16(src_block(i))]

    def height_line(p):
        return 2 * ((p // 2 + iz) % 4) + p % 2

    def to_height(src, dst, phase):
        def go(k, c):
            p = (o + k) % NO
            remote(
                src.at[pl.ds(height_line(p) * 2, 2)], dst.at[:, rows16(o), :], phase, {"outer": p}
            ).start()
            return c

        lax.fori_loop(1, NO, go, 0)
        dst[:, rows16(o), :] = src[pl.ds(height_line(o) * 2, 2)]

    def from_height(src, dst, phase):
        def go(k, c):
            p = (o + k) % NO
            remote(
                src.at[:, rows16(p), :], dst.at[pl.ds(height_line(o) * 2, 2)], phase, {"outer": p}
            ).start()
            return c

        lax.fori_loop(1, NO, go, 0)
        dst[pl.ds(height_line(o) * 2, 2)] = src[:, rows16(o), :]

    def wait_bytes(part, sem):
        pltpu.make_async_copy(part, part, sem).wait()

    def wait_cross(buf, sem):
        @pl.when(same)
        def _():
            wait_bytes(buf.at[pl.ds(0, 63 * 16)], sem)

        @pl.when(jnp.logical_not(same))
        def _():
            wait_bytes(buf, sem)

    wait_wide = lambda buf, sem: wait_bytes(buf.at[pl.ds(0, 31 * 16)], sem)
    wait_outer = lambda buf, sem: wait_bytes(buf.at[pl.ds(0, 14)], sem)

    gain_w = gw_ref[...].astype(F32)
    gain_h = gh_ref[...].astype(F32)
    x = vol_ref[...].astype(F32).reshape(TOK, D)
    s1[...] = pack_wide(x * scale_of(x) * gain_w)
    pl.semaphore_wait(barrier, NI + NO - 2)
    all_inner(s1, r1, 0, block_of, i)

    perms[0] = one_hot(home_to_height, False)
    sx[...] = dot(perms[0], x.astype(BF)).astype(BF).reshape(16, 16, D)
    to_height(sx, rx, 1)
    cot = cot_ref[...].astype(F32).reshape(TOK, D).astype(BF)
    sc[...] = dot(perms[0], cot).astype(BF).reshape(16, 16, D)
    to_height(sc, rc, 2)
    for n, (order, inverse) in enumerate((
        (home_to_height, True), (arrive_to_lines, False), (arrive_to_lines, True), (lines_to_pack, False),
        (lines_to_pack, True), (pack_to_height, False), (pack_to_height, True),
    )):
        perms[n + 1] = one_hot(order, inverse)
    loads[0].wait()
    loads[1].wait()

    wait_wide(r1, recv_sem.at[0])
    lines = dot(perms[2], unpack_wide(r1[...]).astype(BF)).astype(BF)
    proj[...] = dot(lines, qkvw[...]).astype(BF)
    attend(proj, probs, mixed)
    s2[...] = pack_narrow(dot(perms[4], mixed[...]))

    def cross_out(k, c):
        e = k % 2
        kk = k // 2
        dx = 1 - kk // 16
        dz = far_first(kk // 2 % 8)
        dc = 1 - kk % 2
        s = ((ix + dx) % 2) * 16 + ((iz + dz) % 8) * 2 + (ic + dc) % 2
        p = ((frame_w - (s // 2) % 8 + 8) % 4) * 2 + e
        mine = jnp.logical_and(s == i, p == o)
        src = s2.at[rows16(2 * s + e)]
        dst = r2.at[rows16(o * 8 + slot_w)]

        @pl.when(jnp.logical_not(mine))
        def _():
            remote(src, dst, 3, {"outer": p, "inner": s}).start()

        @pl.when(mine)
        def _():
            copy = pltpu.make_async_copy(src, dst, local_sem)
            copy.start()
            copy.wait()

        return c

    lax.fori_loop(0, 64, cross_out, 0)

    loads[2].wait()
    loads[3].wait()
    wait_bytes(rx.at[:, pl.ds(0, 112), :], recv_sem.at[1])
    wait_bytes(rc.at[:, pl.ds(0, 112), :], recv_sem.at[2])
    coth = rc[...].reshape(TOK, D)
    dmixh[...] = dot_nt(coth, outh[...]).astype(BF)

    wait_cross(r2, recv_sem.at[3])
    mixed_here = dot(perms[6], unpack_narrow(r2[...]).astype(BF)).astype(BF)
    middle = (rx[...].reshape(TOK, D).astype(F32) + dot(mixed_here, outw[...])).astype(BF)
    mid[...] = middle
    m32 = middle.astype(F32)
    normed = (m32 * scale_of(m32) * gain_h).astype(BF)
    projh[...] = dot(normed, qkvh[...]).astype(BF)
    attend(projh, probsh, mixedh)
    attend_back(projh, probsh, dmixh, dproj)
    dn = dot_nt(dproj[...], qkvh[...]).astype(BF).astype(F32)
    mgrad = norm_back(mid[...].astype(F32), dn, gain_h, rc[...].reshape(TOK, D).astype(F32)).astype(BF)
    smg[...] = mgrad.reshape(2, 128, D)
    dmw = dot_nt(mgrad, outw[...]).astype(BF)
    s3[...] = pack_narrow(dot(perms[7], dmw))

    def cross_back(k, c):
        p = (o + 7 - k // 8) % 8
        j = (slot_w + k % 8) % 8
        d = device_of(frame_h, j)
        mine = jnp.logical_and(p == o, d == i)
        src = s3.at[rows16(p * 8 + j)]
        dst = r3.at[rows16(2 * i + ol)]

        @pl.when(jnp.logical_not(mine))
        def _():
            remote(src, dst, 4, {"outer": p, "inner": d}).start()

        @pl.when(mine)
        def _():
            copy = pltpu.make_async_copy(src, dst, local_sem)
            copy.start()
            copy.wait()

        return c

    lax.fori_loop(0, 64, cross_back, 0)

    from_height(smg, rmg, 5)
    sres[...] = (mid[...].astype(F32) + dot(mixedh[...], outh[...])).astype(BF).reshape(2, 128, D)
    from_height(sres, rres, 6)

    wait_cross(r3, recv_sem.at[4])
    dmix[...] = dot(perms[5], unpack_narrow(r3[...]).astype(BF)).astype(BF)
    attend_back(proj, probs, dmix, dproj)
    dnw = dot_nt(dproj[...], qkvw[...]).astype(BF)
    s4[...] = pack_wide(dot(perms[3], dnw))
    all_inner(s4, r4, 7, lambda d: d, block_of(i))

    wait_outer(rres, recv_sem.at[6])
    res_ref[...] = dot(perms[1], rres[...].reshape(TOK, D)).reshape(64, 4, D).astype(BF)
    wait_outer(rmg, recv_sem.at[5])
    resid = dot(perms[1], rmg[...].reshape(TOK, D))
    wait_wide(r4, recv_sem.at[7])
    x = vol_ref[...].astype(F32).reshape(TOK, D)
    grad_ref[...] = norm_back(x, unpack_wide(r4[...]), gain_w, resid).reshape(64, 4, D).astype(BF)

    wait_wide(s1, send_sem.at[0])
    wait_outer(sx, send_sem.at[1])
    wait_outer(sc, send_sem.at[2])
    wait_cross(s2, send_sem.at[3])
    wait_cross(s3, send_sem.at[4])
    wait_bytes(smg.at[:, pl.ds(0, 112), :], send_sem.at[5])
    wait_bytes(sres.at[:, pl.ds(0, 112), :], send_sem.at[6])
    wait_wide(s4, send_sem.at[7])


def on_device(volume, cotangent, gain_width, qkv_width, out_width, gain_height, qkv_height, out_height):
    shape = volume.shape
    vm = pl.BlockSpec(memory_space=pltpu.VMEM)
    hbm = pl.BlockSpec(memory_space=pl.ANY)
    flat = jax.ShapeDtypeStruct((64, 4, D), BF)
    v = lambda *s: pltpu.VMEM(s, BF)
    result, grad = pl.pallas_call(
        kernel,
        out_shape=(flat, flat),
        in_specs=[vm, vm, vm, vm, hbm, hbm, hbm, hbm],
        out_specs=(vm, vm),
        scratch_shapes=[
            v(D, 3 * INNER), v(INNER, D), v(D, 3 * INNER), v(INNER, D), v(8, TOK, TOK),
            v(512, 512), v(512, 512), v(1024, 128), v(1024, 128), v(1024, 128), v(1024, 128), v(512, 512), v(512, 512),
            v(16, 16, D), v(2, 128, D), v(16, 16, D), v(2, 128, D),
            v(2, 128, D), v(16, 16, D), v(2, 128, D), v(16, 16, D),
            v(TOK, 3 * INNER), v(TOK, 3 * INNER), pltpu.VMEM((8, TOK, 128), F32), pltpu.VMEM((8, TOK, 128), F32),
            v(TOK, INNER), v(TOK, INNER), v(TOK, 3 * INNER), v(TOK, INNER), v(TOK, INNER), v(TOK, D),
            pltpu.SemaphoreType.DMA((4,)), pltpu.SemaphoreType.DMA((8,)), pltpu.SemaphoreType.DMA((8,)),
            pltpu.SemaphoreType.DMA,
        ],
        compiler_params=pltpu.CompilerParams(
            collective_id=0, has_side_effects=True, vmem_limit_bytes=60 * 1024 * 1024
        ),
    )(
        volume.reshape(64, 4, D), cotangent.reshape(64, 4, D), gain_width.reshape(1, D), gain_height.reshape(1, D),
        qkv_width, out_width, qkv_height, out_height,
    )
    return result.reshape(shape), grad.reshape(shape)


def solution(mesh):
    split = P(None, "outer", "inner", None)
    return jax.shard_map(
        on_device,
        mesh=mesh,
        in_specs=(split, split, P(), P(), P(), P(), P(), P()),
        out_specs=(split, split),
        check_vma=False,
    )
```

time: 255 us -> 80.1 us (0.31); the launches traced: 251 us -> 79.9 us
  Pallas kernels: 0 us -> 72.6 us
  waiting for transfers between devices: 68.2 us -> 0 us
  local copies, waits for them, and re-layouts: 68.9 us -> 6.61 us
  starting transfers between devices: 48.5 us -> 0 us
  matrix products: 31.7 us -> 0 us
  other arithmetic: 20.6 us -> 0 us
  blocking collectives: 12.2 us -> 0 us
    pallas_call x0 -> x1, Pallas kernels: none -> 72.6 us  [on_device(): pl.pallas_call(kernel, out_shape=(flat, flat), in_specs=[vm, vm, vm, vm,...]
    all_to_all x7 -> x0, waiting for transfers between devices: 68.2 us -> none  [the longest x2 32.1 us: from_width(): lax.all_to_all(lines, 'inner', split_axis=1, concat_axis=0, tiled=True)]
    all_to_all x7 -> x0, starting transfers between devices: 48.5 us -> none  [the longest x2 22.8 us: to_width(): lax.all_to_all(block.reshape(frames * rows_h, cols_w, width), 'inner', sp...]
    dot_general x20 -> x0, matrix products: 31.7 us -> none  [the longest x4 9.09 us: sublayer(): jnp.dot(normed.reshape(lines * length, width), qkv, preferred_element_typ...]
    convert_element_type x13 -> x0, local copies, waits for them, and re-layouts: 22.1 us -> none  [the longest x6 9.22 us: sublayer(): values32 = rows.astype(jnp.float32)]
    unnamed x38 -> x2, local copies, waits for them, and re-layouts: 18.4 us -> 4.05 us
    all_to_all x1 -> x0, blocking collectives: 12.2 us -> none  [from_height(): lax.all_to_all(lines, 'outer', split_axis=1, concat_axis=0, tiled=True)]
    reshape x6 -> x2, local copies, waits for them, and re-layouts: 12.8 us -> 2.56 us  [the longest x1 1.28 us: on_device(): gain_width.reshape(1, D)]
  transfers between devices with their start and end apart: 7 -> 0, of which waited for: 5 -> 0; matrix products, arithmetic and copies ran while one was open for 20% -> 0% of each run, Pallas kernels for 0% -> 0%
where the time goes in v1:
time: 80.1 us; the launch traced here: 79.9 us
  Pallas kernels  72.6 us (91%)
  local copies, waits for them, and re-layouts  6.61 us (8%)
    pallas_call x1, Pallas kernels, on_device(): pl.pallas_call(kernel, out_shape=(flat, flat), in_specs=[vm, vm, vm, vm,...  72.6 us
    unnamed x2, local copies, waits for them, and re-layouts  4.05 us

profile of v1, /device:TPU:1, one launch (start us, length us, event | category | flops | bytes accessed | tf_op | source)
XLA Modules:
  0.0 79.9 jit_solution(10551382051161283841)
XLA Ops:
  0.6 1.3 %reshape.24.gw_ref = bf16[1,1024]{1,0:T(2,128)(2,1)} reshape(bf16[1024]{0:T(1024)(128)(2,1)} %param.10) | data formatting | bytes 4096 | tf_op jit(solution)/shard_map/reshape | solution.py:411
  1.9 1.3 %reshape.25.gh_ref = bf16[1,1024]{1,0:T(2,128)(2,1)} reshape(bf16[1024]{0:T(1024)(128)(2,1)} %param.13) | data formatting | bytes 4096 | tf_op jit(solution)/shard_map/reshape | solution.py:411
  3.2 72.6 %shard_map.95 = (bf16[64,4,1024]{2,1,0:T(4,128)(2,1)}, bf16[64,4,1024]{2,1,0:T(4,128)(2,1)}) custom-call(bf16[64,4,1024]{2,1,0:T(4,128)(2,1)} %bitcast.6, bf16[64,4,1024]{2,1,0:T(4,128)(2,1)} %bitcast.7, bf16[1,1024]{1,0:T(2,128)(2,1)} %reshape.24.gw_ref, bf16[1,1024]{1,0:T(2,128)(2,1)} %reshape.25.gh_ref, bf16[1024,1536]{1,0:T(8,128)(2,1)} %qkvw_hbm.1, ...), custom_call_target="tpu_custom_call" | custom-call | tf_op jit(solution)/shard_map/pallas_call | solution.py:392
  75.8 2.0 %copy.12 = bf16[4,16,4,1024]{3,2,1,0:T(4,128)(2,1)} copy(bf16[4,16,4,1024]{3,2,1,0:T(4,128)(2,1)} %bitcast.5) | data formatting | bytes 1048576
  77.9 2.0 %copy.13 = bf16[4,16,4,1024]{3,2,1,0:T(4,128)(2,1)} copy(bf16[4,16,4,1024]{3,2,1,0:T(4,128)(2,1)} %bitcast.4) | data formatting | bytes 1048576

commit v2 on v0

v2 whole, which is shorter than its diff:
```python
import jax
import jax.numpy as jnp
from jax import lax
from jax.experimental import pallas as pl
from jax.experimental.pallas import tpu as pltpu
from jax.sharding import PartitionSpec as P

MESH = pl.DeviceIdType.MESH
BF = jnp.bfloat16
F32 = jnp.float32
D = 1024
INNER = 512
NI = 32
NO = 8
TOK = 256
PAIRS = 4
EPS = 1e-06


def dot(a, b):
    return jnp.dot(a, b, preferred_element_type=F32)


def dot_nt(a, b):
    return lax.dot_general(a, b, (((1,), (1,)), ((), ())), preferred_element_type=F32)


def dot_tn(a, b):
    return lax.dot_general(a, b, (((0,), (0,)), ((), ())), preferred_element_type=F32)


def home_to_height(r):
    return (r // 64) * 64 + ((r % 8) * 2 + (r // 8) % 2) * 4 + (r // 16) % 4


def height_to_home(r):
    return (r // 64) * 64 + (r % 4) * 16 + ((r // 4) % 2) * 8 + (r // 8) % 8


def last_to_first(r):
    return (r % 64) * 2 + r // 64


def first_to_last(r):
    return (r % 2) * 64 + r // 2


def back_to_lines(r):
    return (r % 2) * 128 + ((r // 2) % 64) * 2 + r // 128


def one_hot(order, n):
    row = lax.broadcasted_iota(jnp.int32, (n, n), 0)
    col = lax.broadcasted_iota(jnp.int32, (n, n), 1)
    return jnp.where(col == order(row), 1.0, 0.0).astype(BF)


def in_low(shape, size):
    return (lax.broadcasted_iota(jnp.int32, shape, 1) // size) % 2 == 0


def swap(a, b, size):
    low = in_low(a.shape, size)
    return jnp.where(low, a, pltpu.roll(b, size, 1)), jnp.where(low, pltpu.roll(a, 8 - size, 1), b)


def pack_tokens(rows):
    g = rows.reshape(rows.shape[0] // 8, 8, D)
    return swap(g[:, :, : D // 2], g[:, :, D // 2 :], 4)


def unpack_tokens(a, b):
    a, b = swap(a, b, 4)
    return jnp.concatenate([a, b], axis=2).reshape(a.shape[0] * 8, D)


def turn(q):
    a0, a2 = swap(q[0], q[2], 4)
    a1, a3 = swap(q[1], q[3], 4)
    return swap(a0, a1, 2) + swap(a2, a3, 2)


def pack_pairs(rows):
    g = rows.reshape(16, 8, INNER)
    parts = turn([g[:, :, 128 * q : 128 * q + 128] for q in range(4)])
    return jnp.stack(parts, axis=1).reshape(64, 8, 128).astype(BF)


def unpack_pairs(blocks):
    g = blocks.astype(F32).reshape(16, 4, 8, 128)
    return jnp.concatenate(turn([g[:, q] for q in range(4)]), axis=2).reshape(128, INNER).astype(BF)


def scale_of(v):
    return lax.rsqrt(jnp.mean(v * v, axis=-1, keepdims=True) + EPS)


def norm_back(v, dn, gain, resid):
    r = scale_of(v)
    gd = dn * gain
    c = jnp.sum(gd * v, axis=-1, keepdims=True) * (1.0 / D)
    return r * gd - v * (r * r * r * c) + resid


def lane_low():
    return lax.broadcasted_iota(jnp.int32, (128, 128), 1) < 64


def two_heads(a):
    low = lane_low()
    zero = jnp.zeros_like(a)
    return jnp.concatenate([jnp.where(low, a, zero), jnp.where(low, zero, a)], axis=0)


def one_pair(a):
    return jnp.where(lane_low(), a[:128], a[128:])


def unit_slices(line, pair):
    rows = pl.ds(line * 128, 128)
    return rows, [pl.ds(INNER * part + 128 * pair, 128) for part in range(3)]


def attend(proj, probs, mixed, line):
    for pair in range(PAIRS):
        rows, (qs, ks, vs) = unit_slices(line, pair)
        s = dot_nt(two_heads(proj[rows, qs]), proj[rows, ks]) * 0.125
        e = jnp.exp(s - jnp.max(s, axis=-1, keepdims=True))
        p = e / jnp.sum(e, axis=-1, keepdims=True)
        probs[line * PAIRS + pair] = p
        mixed[rows, pl.ds(128 * pair, 128)] = one_pair(dot(p.astype(BF), proj[rows, vs])).astype(BF)


def attend_back(proj, probs, dmixed, dproj, line):
    for pair in range(PAIRS):
        rows, (qs, ks, vs) = unit_slices(line, pair)
        p = probs[line * PAIRS + pair]
        do = two_heads(dmixed[rows, pl.ds(128 * pair, 128)])
        dp = dot_nt(do, proj[rows, vs]).astype(BF).astype(F32)
        dproj[rows, vs] = dot_tn(p.astype(BF), do).astype(BF)
        ds = p * (dp - jnp.sum(dp * p, axis=-1, keepdims=True)) * 0.125
        ds = ds.astype(BF)
        dproj[rows, qs] = one_pair(dot(ds, proj[rows, ks])).astype(BF)
        dproj[rows, ks] = dot_tn(ds, two_heads(proj[rows, qs])).astype(BF)


FAR_FIRST = (4, 3, 5, 2, 6, 1, 7, 0)


def kernel(
    vol_ref, cot_ref, gw_ref, gh_ref, qkvw_hbm, outw_hbm, qkvh_hbm, outh_hbm,
    res_ref, grad_ref,
    qkvw, outw, qkvh, outh, perms, halves,
    s1, r1, s2, r2, s3, r3, s4, r4,
    sx, rx, sc, rc, sres, rres, smg, rmg,
    proj, projh, probs, probsh, mixed, mixedh, dproj, dmix, dmixh, mid,
    load_sem, send_sem, recv_sem, local_sem,
):
    i = lax.axis_index("inner")
    o = lax.axis_index("outer")
    ix, iz, ic = i // 16, (i // 2) % 8, i % 2
    oy, ol = o // 2, o % 2
    frame_w = ix * 2 + iz % 2
    slot_w = (iz // 2) * 2 + ic
    frame_h = (oy + iz) % 4
    same = frame_w == frame_h
    xs = (ix, (ix + 1) % 2)
    zs = [(iz + d) % 8 for d in range(8)]
    cs = (ic, (ic + 1) % 2)

    loads = [
        pltpu.make_async_copy(a, b, load_sem.at[n])
        for n, (a, b) in enumerate(((qkvw_hbm, qkvw), (outh_hbm, outh), (outw_hbm, outw), (qkvh_hbm, qkvh)))
    ]
    for load in loads:
        load.start()

    barrier = pltpu.get_barrier_semaphore()

    def greet_inner(k, c):
        pl.semaphore_signal(barrier, inc=1, device_id={"inner": (i + k) % NI}, device_id_type=MESH)
        return c

    def greet_outer(k, c):
        pl.semaphore_signal(barrier, inc=1, device_id={"outer": (o + k) % NO}, device_id_type=MESH)
        return c

    lax.fori_loop(1, NI, greet_inner, 0)
    lax.fori_loop(1, NO, greet_outer, 0)

    def remote(src, dst, sem, target):
        pltpu.make_async_remote_copy(
            src_ref=src, dst_ref=dst, send_sem=send_sem.at[sem], recv_sem=recv_sem.at[sem],
            device_id=target, device_id_type=MESH,
        ).start()

    def local(src, dst):
        copy = pltpu.make_async_copy(src, dst, local_sem)
        copy.start()
        copy.wait()

    def block(x, z, c):
        return (x * 2 + z % 2) * 8 + (z // 2) * 2 + c

    def to_width(half):
        for dx in (1, 0):
            for dz in FAR_FIRST:
                for dc in (1, 0):
                    x, z, c = xs[dx], zs[dz], cs[dc]
                    src, dst = s1.at[half, block(x, z, c)], r1.at[half, i]
                    if dx or dz or dc:
                        remote(src, dst, half, {"inner": x * 16 + z * 2 + c})
                    else:
                        local(src, dst)

    def from_width(half):
        for dx in (1, 0):
            for dz in FAR_FIRST:
                for dc in (1, 0):
                    d = xs[dx] * 16 + zs[dz] * 2 + cs[dc]
                    src, dst = s4.at[half, d], r4.at[half, block(ix, iz, ic)]
                    if dx or dz or dc:
                        remote(src, dst, 6 + half, {"inner": d})
                    else:
                        local(src, dst)

    def width_to_height(half):
        for dx in (1, 0):
            for dz in FAR_FIRST:
                y = (frame_w + 8 - zs[dz]) % 4
                for dc in (1, 0):
                    for e in (0, 1):
                        s = xs[dx] * 16 + zs[dz] * 2 + cs[dc]
                        p = y * 2 + e
                        src, dst = s2.at[half, 2 * s + e], r2.at[half, o * 8 + slot_w]
                        if dx or dz or dc:
                            remote(src, dst, 2 + half, {"outer": p, "inner": s})
                        else:
                            pl.when(p != o)(lambda src=src, dst=dst, p=p, s=s: remote(src, dst, 2 + half, {"outer": p, "inner": s}))
                            pl.when(p == o)(lambda src=src, dst=dst: local(src, dst))

    def height_to_width(half):
        base = (frame_h // 2) * 16 + (frame_h % 2) * 2
        js = [(slot_w + k) % 8 for k in range(8)]
        ds = [base + (j // 2) * 4 + j % 2 for j in js]
        for dp in (7, 6, 5, 4, 3, 2, 1, 0):
            p = (o + dp) % 8
            for k in range(8):
                src, dst = s3.at[half, p * 8 + js[k]], r3.at[half, 2 * i + ol]
                if dp or k:
                    remote(src, dst, 4 + half, {"outer": p, "inner": ds[k]})
                else:
                    pl.when(ds[k] != i)(lambda src=src, dst=dst, p=p, d=ds[k]: remote(src, dst, 4 + half, {"outer": p, "inner": d}))
                    pl.when(ds[k] == i)(lambda src=src, dst=dst: local(src, dst))

    def height_line(p):
        return 2 * ((p // 2 + iz) % 4) + p % 2

    def to_height(src, dst, sem):
        def go(k, c):
            p = (o + k) % NO
            remote(src.at[pl.ds(height_line(p) * 2, 2)], dst.at[:, :, o], sem, {"outer": p})
            return c

        lax.fori_loop(1, NO, go, 0)
        local(src.at[pl.ds(height_line(o) * 2, 2)], dst.at[:, :, o])

    def from_height(src, dst, sem):
        def go(k, c):
            p = (o + k) % NO
            remote(src.at[:, :, p], dst.at[pl.ds(height_line(o) * 2, 2)], sem, {"outer": p})
            return c

        lax.fori_loop(1, NO, go, 0)
        local(src.at[:, :, o], dst.at[pl.ds(height_line(o) * 2, 2)])

    def wait_bytes(part, sem):
        pltpu.make_async_copy(part, part, sem).wait()

    def wait_inner(buf, half, sem):
        wait_bytes(buf.at[half, pl.ds(0, 31)], sem)

    def wait_cross(buf, half, sem):
        pl.when(same)(lambda: wait_bytes(buf.at[half, pl.ds(0, 63)], sem))
        pl.when(jnp.logical_not(same))(lambda: wait_bytes(buf.at[half], sem))

    def wait_lines(buf, sem):
        wait_bytes(buf.at[:, :, pl.ds(0, 7)], sem)

    def wait_home(buf, sem):
        wait_bytes(buf.at[pl.ds(0, 14)], sem)

    gain_w = gw_ref[...].astype(F32).reshape(1, D)
    gain_h = gh_ref[...].astype(F32).reshape(1, D)
    x = vol_ref[...].astype(F32).reshape(TOK, D)
    first, second = pack_tokens(x * scale_of(x) * gain_w)
    s1[0] = first.astype(BF)
    s1[1] = second.astype(BF)
    pl.semaphore_wait(barrier, NI + NO - 2)
    to_width(0)
    to_width(1)

    perms[0] = one_hot(home_to_height, TOK)
    sx[...] = dot(perms[0], x.astype(BF)).astype(BF).reshape(16, 2, 8, D)
    to_height(sx, rx, 8)
    cot = cot_ref[...].astype(F32).reshape(TOK, D).astype(BF)
    sc[...] = dot(perms[0], cot).astype(BF).reshape(16, 2, 8, D)
    to_height(sc, rc, 9)
    perms[1] = one_hot(height_to_home, TOK)
    perms[2] = one_hot(back_to_lines, TOK)
    halves[0] = one_hot(last_to_first, 128)
    halves[1] = one_hot(first_to_last, 128)
    loads[0].wait()
    loads[1].wait()

    for line in range(2):
        rows = pl.ds(line * 128, 128)
        wait_inner(r1, line, recv_sem.at[line])
        got = r1[line].astype(F32).reshape(16, 2, 8, D // 2)
        tokens = unpack_tokens(got[:, 0], got[:, 1]).astype(BF)
        proj[rows] = dot(tokens, qkvw[...]).astype(BF)
        attend(proj, probs, mixed, line)
        s2[line] = pack_pairs(mixed[rows].astype(F32))
        width_to_height(line)

    loads[2].wait()
    loads[3].wait()
    wait_lines(rx, recv_sem.at[8])
    wait_lines(rc, recv_sem.at[9])
    dmixh[...] = dot_nt(rc[...].reshape(TOK, D), outh[...]).astype(BF)

    for half in range(2):
        wait_cross(r2, half, recv_sem.at[2 + half])
        here = dot(halves[0], unpack_pairs(r2[half])).astype(BF)
        middle = (rx[:, half].astype(F32).reshape(128, D) + dot(here, outw[...])).astype(BF)
        m32 = middle.astype(F32)
        normed = (m32 * scale_of(m32) * gain_h).astype(BF)
        got = dot(normed, qkvh[...]).astype(BF)
        for line in range(2):
            rows = pl.ds(line * 128 + half * 64, 64)
            mid[rows] = middle[line * 64 : line * 64 + 64]
            projh[rows] = got[line * 64 : line * 64 + 64]
    for line in range(2):
        rows = pl.ds(line * 128, 128)
        attend(projh, probsh, mixedh, line)
        attend_back(projh, probsh, dmixh, dproj, line)
        dn = dot_nt(dproj[rows], qkvh[...]).astype(BF).astype(F32)
        resid = rc[line].astype(F32).reshape(128, D)
        mgrad = norm_back(mid[rows].astype(F32), dn, gain_h, resid).astype(BF)
        smg[line] = mgrad.reshape(2, 8, 8, D)
        dmw = dot_nt(mgrad, outw[...]).astype(BF)
        s3[line] = pack_pairs(dot(halves[1], dmw))
        height_to_width(line)
    from_height(smg, rmg, 10)
    sres[...] = (mid[...].astype(F32) + dot(mixedh[...], outh[...])).astype(BF).reshape(2, 2, 8, 8, D)
    from_height(sres, rres, 11)

    wait_cross(r3, 0, recv_sem.at[4])
    wait_cross(r3, 1, recv_sem.at[5])
    back = jnp.concatenate([unpack_pairs(r3[0]), unpack_pairs(r3[1])], axis=0)
    dmix[...] = dot(perms[2], back).astype(BF)
    for line in range(2):
        rows = pl.ds(line * 128, 128)
        attend_back(proj, probs, dmix, dproj, line)
        dn = dot_nt(dproj[rows], qkvw[...]).astype(BF).astype(F32)
        s4[line] = jnp.stack(pack_tokens(dn), axis=1).reshape(NI, 8, D // 2).astype(BF)
        from_width(line)

    wait_home(rres, recv_sem.at[11])
    res_ref[...] = dot(perms[1], rres[...].reshape(TOK, D)).reshape(64, 4, D).astype(BF)
    wait_home(rmg, recv_sem.at[10])
    resid = dot(perms[1], rmg[...].reshape(TOK, D))
    wait_inner(r4, 0, recv_sem.at[6])
    wait_inner(r4, 1, recv_sem.at[7])
    x = vol_ref[...].astype(F32).reshape(TOK, D)
    dn = unpack_tokens(r4[0].astype(F32), r4[1].astype(F32))
    grad_ref[...] = norm_back(x, dn, gain_w, resid).reshape(64, 4, D).astype(BF)

    for half in range(2):
        wait_inner(s1, half, send_sem.at[half])
        wait_cross(s2, half, send_sem.at[2 + half])
        wait_cross(s3, half, send_sem.at[4 + half])
        wait_inner(s4, half, send_sem.at[6 + half])
    wait_home(sx, send_sem.at[8])
    wait_home(sc, send_sem.at[9])
    wait_lines(smg, send_sem.at[10])
    wait_lines(sres, send_sem.at[11])


def hand_over(a_ref, b_ref, x_ref, y_ref):
    x_ref[...] = a_ref[...]
    y_ref[...] = b_ref[...]


def on_device(volume, cotangent, gain_width, qkv_width, out_width, gain_height, qkv_height, out_height):
    shape = volume.shape
    vm = pl.BlockSpec(memory_space=pltpu.VMEM)
    hbm = pl.BlockSpec(memory_space=pl.ANY)
    flat = jax.ShapeDtypeStruct((64, 4, D), BF)
    v = lambda *s: pltpu.VMEM(s, BF)
    result, grad = pl.pallas_call(
        kernel,
        out_shape=(flat, flat),
        in_specs=[vm, vm, vm, vm, hbm, hbm, hbm, hbm],
        out_specs=(vm, vm),
        scratch_shapes=[
            v(D, 3 * INNER), v(INNER, D), v(D, 3 * INNER), v(INNER, D), v(3, TOK, TOK), v(2, 128, 128),
            v(2, 32, 8, 512), v(2, 32, 8, 512), v(2, 64, 8, 128), v(2, 64, 8, 128),
            v(2, 64, 8, 128), v(2, 64, 8, 128), v(2, 32, 8, 512), v(2, 32, 8, 512),
            v(16, 2, 8, D), v(2, 2, 8, 8, D), v(16, 2, 8, D), v(2, 2, 8, 8, D),
            v(2, 2, 8, 8, D), v(16, 2, 8, D), v(2, 2, 8, 8, D), v(16, 2, 8, D),
            v(TOK, 3 * INNER), v(TOK, 3 * INNER), pltpu.VMEM((8, TOK, 128), F32), pltpu.VMEM((8, TOK, 128), F32),
            v(TOK, INNER), v(TOK, INNER), v(TOK, 3 * INNER), v(TOK, INNER), v(TOK, INNER), v(TOK, D),
            pltpu.SemaphoreType.DMA((4,)), pltpu.SemaphoreType.DMA((12,)), pltpu.SemaphoreType.DMA((12,)),
            pltpu.SemaphoreType.DMA,
        ],
        compiler_params=pltpu.CompilerParams(
            collective_id=0, has_side_effects=True, vmem_limit_bytes=60 * 1024 * 1024
        ),
    )(
        volume.reshape(64, 4, D), cotangent.reshape(64, 4, D), gain_width, gain_height,
        qkv_width, out_width, qkv_height, out_height,
    )
    result, grad = pl.pallas_call(hand_over, out_shape=(flat, flat), in_specs=[vm, vm], out_specs=(vm, vm))(result, grad)
    return result.reshape(shape), grad.reshape(shape)


def solution(mesh):
    split = P(None, "outer", "inner", None)
    return jax.shard_map(
        on_device,
        mesh=mesh,
        in_specs=(split, split, P(), P(), P(), P(), P(), P()),
        out_specs=(split, split),
        check_vma=False,
    )
```

time: 255 us -> 74.5 us (0.29); the launches traced: 251 us -> 74.4 us
  Pallas kernels: 0 us -> 73.7 us
  local copies, waits for them, and re-layouts: 68.9 us -> 0 us
  waiting for transfers between devices: 68.2 us -> 0 us
  starting transfers between devices: 48.5 us -> 0 us
  matrix products: 31.7 us -> 0 us
  other arithmetic: 20.6 us -> 0 us
  blocking collectives: 12.2 us -> 0 us
    pallas_call x0 -> x2, Pallas kernels: none -> 73.7 us  [the longest x1 71.5 us: on_device(): pl.pallas_call(kernel, out_shape=(flat, flat), in_specs=[vm, vm, vm, vm,...]
    all_to_all x7 -> x0, waiting for transfers between devices: 68.2 us -> none  [the longest x2 32.1 us: from_width(): lax.all_to_all(lines, 'inner', split_axis=1, concat_axis=0, tiled=True)]
    all_to_all x7 -> x0, starting transfers between devices: 48.5 us -> none  [the longest x2 22.8 us: to_width(): lax.all_to_all(block.reshape(frames * rows_h, cols_w, width), 'inner', sp...]
    dot_general x20 -> x0, matrix products: 31.7 us -> none  [the longest x4 9.09 us: sublayer(): jnp.dot(normed.reshape(lines * length, width), qkv, preferred_element_typ...]
    convert_element_type x13 -> x0, local copies, waits for them, and re-layouts: 22.1 us -> none  [the longest x6 9.22 us: sublayer(): values32 = rows.astype(jnp.float32)]
    unnamed x38 -> x0, local copies, waits for them, and re-layouts: 18.4 us -> none
    reshape x6 -> x0, local copies, waits for them, and re-layouts: 12.8 us -> none  [the longest x2 6.12 us: sublayer(): proj = proj.reshape(lines, length, 3, heads, hdim)]
    all_to_all x1 -> x0, blocking collectives: 12.2 us -> none  [from_height(): lax.all_to_all(lines, 'outer', split_axis=1, concat_axis=0, tiled=True)]
  transfers between devices with their start and end apart: 7 -> 0, of which waited for: 5 -> 0; matrix products, arithmetic and copies ran while one was open for 20% -> 0% of each run, Pallas kernels for 0% -> 0%
where the time goes in v2:
time: 74.5 us; the launch traced here: 74.4 us
  Pallas kernels  73.7 us (99%)
    pallas_call x1, Pallas kernels, on_device(): pl.pallas_call(kernel, out_shape=(flat, flat), in_specs=[vm, vm, vm, vm,...  71.5 us
    pallas_call x1, Pallas kernels, on_device(): pl.pallas_call(hand_over, out_shape=(flat, flat), in_specs=[vm, vm], out_...  2.2 us

profile of v2, /device:TPU:1, one launch (start us, length us, event | category | flops | bytes accessed | tf_op | source)
XLA Modules:
  0.0 74.4 jit_solution(7817306150350950317)
XLA Ops:
  0.6 71.5 %shard_map.95 = (bf16[64,4,1024]{2,1,0:T(4,128)(2,1)}, bf16[64,4,1024]{2,1,0:T(4,128)(2,1)}) custom-call(bf16[64,4,1024]{2,1,0:T(4,128)(2,1)} %bitcast.4, bf16[64,4,1024]{2,1,0:T(4,128)(2,1)} %bitcast.5, bf16[1024]{0:T(1024)(128)(2,1)} %gw_ref.1, bf16[1024]{0:T(1024)(128)(2,1)} %gh_ref.1, bf16[1024,1536]{1,0:T(8,128)(2,1)} %qkvw_hbm.1, ...), custom_call_target="tpu_custom_call" | custom-call | tf_op jit(solution)/shard_map/pallas_call | solution.py:401
  72.2 2.2 %shard_map.96 = (bf16[64,4,1024]{2,1,0:T(4,128)(2,1)}, bf16[64,4,1024]{2,1,0:T(4,128)(2,1)}) custom-call(bf16[64,4,1024]{2,1,0:T(4,128)(2,1)} %get-tuple-element.6.a_ref, bf16[64,4,1024]{2,1,0:T(4,128)(2,1)} %get-tuple-element.7.b_ref), custom_call_target="tpu_custom_call" | custom-call | tf_op jit(solution)/shard_map/pallas_call | solution.py:424

commit v3 on v2

--- a/solution.py
+++ b/solution.py
@@ -41,12 +41,12 @@
     return (r % 64) * 2 + r // 64
 
 
-def first_to_last(r):
-    return (r % 2) * 64 + r // 2
-
-
 def back_to_lines(r):
-    return (r % 2) * 128 + ((r // 2) % 64) * 2 + r // 128
+    return ((r // 2) % 64) * 4 + (r // 128) * 2 + r % 2
+
+
+def lines_to_back(r):
+    return (r % 2) * 128 + ((r // 2) % 2) * 64 + r // 4
 
 
 def one_hot(order, n):
@@ -89,6 +89,19 @@
 def unpack_pairs(blocks):
     g = blocks.astype(F32).reshape(16, 4, 8, 128)
     return jnp.concatenate(turn([g[:, q] for q in range(4)]), axis=2).reshape(128, INNER).astype(BF)
+
+
+def pack_fours(rows):
+    g = rows.reshape(32, 8, INNER)
+    q = [g[:, :, 128 * k : 128 * k + 128] for k in range(4)]
+    (a0, b0), (a1, b1) = swap(q[0], q[1], 4), swap(q[2], q[3], 4)
+    return jnp.stack((a0, a1, b0, b1), axis=1).reshape(64, 16, 128).astype(BF)
+
+
+def unpack_fours(blocks):
+    g = blocks.astype(F32).reshape(32, 4, 8, 128)
+    parts = swap(g[:, 0], g[:, 2], 4) + swap(g[:, 1], g[:, 3], 4)
+    return jnp.concatenate(parts, axis=2).reshape(TOK, INNER).astype(BF)
 
 
 def scale_of(v):
@@ -126,7 +139,7 @@
         rows, (qs, ks, vs) = unit_slices(line, pair)
         s = dot_nt(two_heads(proj[rows, qs]), proj[rows, ks]) * 0.125
         e = jnp.exp(s - jnp.max(s, axis=-1, keepdims=True))
-        p = e / jnp.sum(e, axis=-1, keepdims=True)
+        p = e * (1.0 / jnp.sum(e, axis=-1, keepdims=True))
         probs[line * PAIRS + pair] = p
         mixed[rows, pl.ds(128 * pair, 128)] = one_pair(dot(p.astype(BF), proj[rows, vs])).astype(BF)
 
@@ -148,19 +161,19 @@
 
 
 def kernel(
-    vol_ref, cot_ref, gw_ref, gh_ref, qkvw_hbm, outw_hbm, qkvh_hbm, outh_hbm,
-    res_ref, grad_ref,
-    qkvw, outw, qkvh, outh, perms, halves,
+    vol_hbm, cot_hbm, gw_hbm, gh_hbm, qkvw_hbm, outw_hbm, qkvh_hbm, outh_hbm,
+    res_hbm, grad_hbm,
+    vol_ref, cot_ref, res_ref, grad_ref, gw_ref, gh_ref, qkvw, outw, qkvh, outh, perms, halves,
     s1, r1, s2, r2, s3, r3, s4, r4,
     sx, rx, sc, rc, sres, rres, smg, rmg,
     proj, projh, probs, probsh, mixed, mixedh, dproj, dmix, dmixh, mid,
-    load_sem, send_sem, recv_sem, local_sem,
+    load_sem, store_sem, send_sem, recv_sem, local_sem,
 ):
     i = lax.axis_index("inner")
     o = lax.axis_index("outer")
     ix, iz, ic = i // 16, (i // 2) % 8, i % 2
     oy, ol = o // 2, o % 2
-    frame_w = ix * 2 + iz % 2
+    frame_w = (iz % 2) * 2 + ix
     slot_w = (iz // 2) * 2 + ic
     frame_h = (oy + iz) % 4
     same = frame_w == frame_h
@@ -168,25 +181,20 @@
     zs = [(iz + d) % 8 for d in range(8)]
     cs = (ic, (ic + 1) % 2)
 
-    loads = [
-        pltpu.make_async_copy(a, b, load_sem.at[n])
-        for n, (a, b) in enumerate(((qkvw_hbm, qkvw), (outh_hbm, outh), (outw_hbm, outw), (qkvh_hbm, qkvh)))
-    ]
-    for load in loads:
-        load.start()
-
     barrier = pltpu.get_barrier_semaphore()
-
-    def greet_inner(k, c):
-        pl.semaphore_signal(barrier, inc=1, device_id={"inner": (i + k) % NI}, device_id_type=MESH)
-        return c
-
-    def greet_outer(k, c):
-        pl.semaphore_signal(barrier, inc=1, device_id={"outer": (o + k) % NO}, device_id_type=MESH)
-        return c
-
-    lax.fori_loop(1, NI, greet_inner, 0)
-    lax.fori_loop(1, NO, greet_outer, 0)
+    for dx in (1, 0):
+        for dz in FAR_FIRST:
+            for dc in (1, 0):
+                if dx or dz or dc:
+                    greeted = {"inner": xs[dx] * 16 + zs[dz] * 2 + cs[dc]}
+                    pl.semaphore_signal(barrier, inc=1, device_id=greeted, device_id_type=MESH)
+    for dp in range(1, NO):
+        pl.semaphore_signal(barrier, inc=1, device_id={"outer": (o + dp) % NO}, device_id_type=MESH)
+
+    moves = ((vol_hbm, vol_ref), (cot_hbm, cot_ref), (qkvw_hbm, qkvw), (outh_hbm, outh), (outw_hbm, outw), (qkvh_hbm, qkvh), (gw_hbm, gw_ref), (gh_hbm, gh_ref))
+    loads = [pltpu.make_async_copy(a, b, load_sem.at[n]) for n, (a, b) in enumerate(moves)]
+    for n in (0, 6, 7, 1, 2, 3, 4, 5):
+        loads[n].start()
 
     def remote(src, dst, sem, target):
         pltpu.make_async_remote_copy(
@@ -200,18 +208,24 @@
         copy.wait()
 
     def block(x, z, c):
-        return (x * 2 + z % 2) * 8 + (z // 2) * 2 + c
-
-    def to_width(half):
-        for dx in (1, 0):
-            for dz in FAR_FIRST:
-                for dc in (1, 0):
-                    x, z, c = xs[dx], zs[dz], cs[dc]
-                    src, dst = s1.at[half, block(x, z, c)], r1.at[half, i]
-                    if dx or dz or dc:
-                        remote(src, dst, half, {"inner": x * 16 + z * 2 + c})
-                    else:
-                        local(src, dst)
+        return ((z % 2) * 2 + x) * 8 + (z // 2) * 2 + c
+
+    def to_width():
+        for odd in (0, 1):
+            turned = (iz + odd) % 2
+            far = [(iz + a + turned * (b - a)) % 8 for a, b in ((4, 3), (2, 5), (6, 1), (0, 7))]
+            for half in (0, 1):
+                for dx in (1, 0):
+                    for k, z in enumerate(far):
+                        for dc in (1, 0):
+                            x, c = xs[dx], cs[dc]
+                            src, dst = s1.at[half, block(x, z, c)], r1.at[half, i]
+                            send = lambda src=src, dst=dst, d=x * 16 + z * 2 + c, half=half: remote(src, dst, half, {"inner": d})
+                            if dx or dc or k < 3:
+                                send()
+                            else:
+                                pl.when(turned != 0)(send)
+                                pl.when(turned == 0)(lambda src=src, dst=dst: local(src, dst))
 
     def from_width(half):
         for dx in (1, 0):
@@ -239,18 +253,18 @@
                             pl.when(p != o)(lambda src=src, dst=dst, p=p, s=s: remote(src, dst, 2 + half, {"outer": p, "inner": s}))
                             pl.when(p == o)(lambda src=src, dst=dst: local(src, dst))
 
-    def height_to_width(half):
-        base = (frame_h // 2) * 16 + (frame_h % 2) * 2
+    def height_to_width():
+        base = (frame_h % 2) * 16 + (frame_h // 2) * 2
         js = [(slot_w + k) % 8 for k in range(8)]
         ds = [base + (j // 2) * 4 + j % 2 for j in js]
         for dp in (7, 6, 5, 4, 3, 2, 1, 0):
             p = (o + dp) % 8
             for k in range(8):
-                src, dst = s3.at[half, p * 8 + js[k]], r3.at[half, 2 * i + ol]
+                src, dst = s3.at[p * 8 + js[k]], r3.at[2 * i + ol]
                 if dp or k:
-                    remote(src, dst, 4 + half, {"outer": p, "inner": ds[k]})
+                    remote(src, dst, 4, {"outer": p, "inner": ds[k]})
                 else:
-                    pl.when(ds[k] != i)(lambda src=src, dst=dst, p=p, d=ds[k]: remote(src, dst, 4 + half, {"outer": p, "inner": d}))
+                    pl.when(ds[k] != i)(lambda src=src, dst=dst, p=p, d=ds[k]: remote(src, dst, 4, {"outer": p, "inner": d}))
                     pl.when(ds[k] == i)(lambda src=src, dst=dst: local(src, dst))
 
     def height_line(p):
@@ -280,6 +294,10 @@
     def wait_inner(buf, half, sem):
         wait_bytes(buf.at[half, pl.ds(0, 31)], sem)
 
+    def wait_back(buf, sem):
+        pl.when(same)(lambda: wait_bytes(buf.at[pl.ds(0, 63)], sem))
+        pl.when(jnp.logical_not(same))(lambda: wait_bytes(buf, sem))
+
     def wait_cross(buf, half, sem):
         pl.when(same)(lambda: wait_bytes(buf.at[half, pl.ds(0, 63)], sem))
         pl.when(jnp.logical_not(same))(lambda: wait_bytes(buf.at[half], sem))
@@ -290,28 +308,31 @@
     def wait_home(buf, sem):
         wait_bytes(buf.at[pl.ds(0, 14)], sem)
 
+    loads[6].wait()
+    loads[7].wait()
     gain_w = gw_ref[...].astype(F32).reshape(1, D)
     gain_h = gh_ref[...].astype(F32).reshape(1, D)
+    loads[0].wait()
     x = vol_ref[...].astype(F32).reshape(TOK, D)
     first, second = pack_tokens(x * scale_of(x) * gain_w)
     s1[0] = first.astype(BF)
     s1[1] = second.astype(BF)
     pl.semaphore_wait(barrier, NI + NO - 2)
-    to_width(0)
-    to_width(1)
+    to_width()
 
     perms[0] = one_hot(home_to_height, TOK)
     sx[...] = dot(perms[0], x.astype(BF)).astype(BF).reshape(16, 2, 8, D)
     to_height(sx, rx, 8)
+    loads[1].wait()
     cot = cot_ref[...].astype(F32).reshape(TOK, D).astype(BF)
     sc[...] = dot(perms[0], cot).astype(BF).reshape(16, 2, 8, D)
     to_height(sc, rc, 9)
     perms[1] = one_hot(height_to_home, TOK)
     perms[2] = one_hot(back_to_lines, TOK)
-    halves[0] = one_hot(last_to_first, 128)
-    halves[1] = one_hot(first_to_last, 128)
-    loads[0].wait()
-    loads[1].wait()
+    halves[...] = one_hot(last_to_first, 128)
+    perms[3] = one_hot(lines_to_back, TOK)
+    loads[2].wait()
+    loads[3].wait()
 
     for line in range(2):
         rows = pl.ds(line * 128, 128)
@@ -323,15 +344,15 @@
         s2[line] = pack_pairs(mixed[rows].astype(F32))
         width_to_height(line)
 
-    loads[2].wait()
-    loads[3].wait()
+    loads[4].wait()
+    loads[5].wait()
     wait_lines(rx, recv_sem.at[8])
     wait_lines(rc, recv_sem.at[9])
     dmixh[...] = dot_nt(rc[...].reshape(TOK, D), outh[...]).astype(BF)
 
     for half in range(2):
         wait_cross(r2, half, recv_sem.at[2 + half])
-        here = dot(halves[0], unpack_pairs(r2[half])).astype(BF)
+        here = dot(halves[...], unpack_pairs(r2[half])).astype(BF)
         middle = (rx[:, half].astype(F32).reshape(128, D) + dot(here, outw[...])).astype(BF)
         m32 = middle.astype(F32)
         normed = (m32 * scale_of(m32) * gain_h).astype(BF)
@@ -341,24 +362,20 @@
             mid[rows] = middle[line * 64 : line * 64 + 64]
             projh[rows] = got[line * 64 : line * 64 + 64]
     for line in range(2):
-        rows = pl.ds(line * 128, 128)
         attend(projh, probsh, mixedh, line)
         attend_back(projh, probsh, dmixh, dproj, line)
-        dn = dot_nt(dproj[rows], qkvh[...]).astype(BF).astype(F32)
-        resid = rc[line].astype(F32).reshape(128, D)
-        mgrad = norm_back(mid[rows].astype(F32), dn, gain_h, resid).astype(BF)
-        smg[line] = mgrad.reshape(2, 8, 8, D)
-        dmw = dot_nt(mgrad, outw[...]).astype(BF)
-        s3[line] = pack_pairs(dot(halves[1], dmw))
-        height_to_width(line)
+    dn = dot_nt(dproj[...], qkvh[...]).astype(BF).astype(F32)
+    mgrad = norm_back(mid[...].astype(F32), dn, gain_h, rc[...].astype(F32).reshape(TOK, D)).astype(BF)
+    smg[...] = mgrad.reshape(2, 2, 8, 8, D)
+    dmw = dot_nt(mgrad, outw[...]).astype(BF)
+    s3[...] = pack_fours(dot(perms[3], dmw))
+    height_to_width()
     from_height(smg, rmg, 10)
     sres[...] = (mid[...].astype(F32) + dot(mixedh[...], outh[...])).astype(BF).reshape(2, 2, 8, 8, D)
     from_height(sres, rres, 11)
 
-    wait_cross(r3, 0, recv_sem.at[4])
-    wait_cross(r3, 1, recv_sem.at[5])
-    back = jnp.concatenate([unpack_pairs(r3[0]), unpack_pairs(r3[1])], axis=0)
-    dmix[...] = dot(perms[2], back).astype(BF)
+    wait_back(r3, recv_sem.at[4])
+    dmix[...] = dot(perms[2], unpack_fours(r3[...])).astype(BF)
     for line in range(2):
         rows = pl.ds(line * 128, 128)
         attend_back(proj, probs, dmix, dproj, line)
@@ -368,6 +385,11 @@
 
     wait_home(rres, recv_sem.at[11])
     res_ref[...] = dot(perms[1], rres[...].reshape(TOK, D)).reshape(64, 4, D).astype(BF)
+    stores = [
+        pltpu.make_async_copy(a, b, store_sem.at[n])
+        for n, (a, b) in enumerate(((res_ref, res_hbm), (grad_ref, grad_hbm)))
+    ]
+    stores[0].start()
     wait_home(rmg, recv_sem.at[10])
     resid = dot(perms[1], rmg[...].reshape(TOK, D))
     wait_inner(r4, 0, recv_sem.at[6])
@@ -375,43 +397,58 @@
     x = vol_ref[...].astype(F32).reshape(TOK, D)
     dn = unpack_tokens(r4[0].astype(F32), r4[1].astype(F32))
     grad_ref[...] = norm_back(x, dn, gain_w, resid).reshape(64, 4, D).astype(BF)
+    stores[1].start()
 
     for half in range(2):
         wait_inner(s1, half, send_sem.at[half])
         wait_cross(s2, half, send_sem.at[2 + half])
-        wait_cross(s3, half, send_sem.at[4 + half])
         wait_inner(s4, half, send_sem.at[6 + half])
+    wait_back(s3, send_sem.at[4])
     wait_home(sx, send_sem.at[8])
     wait_home(sc, send_sem.at[9])
     wait_lines(smg, send_sem.at[10])
     wait_lines(sres, send_sem.at[11])
-
-
-def hand_over(a_ref, b_ref, x_ref, y_ref):
-    x_ref[...] = a_ref[...]
-    y_ref[...] = b_ref[...]
+    stores[0].wait()
+    stores[1].wait()
+
+
+def hand_over(a_hbm, b_hbm, x_hbm, y_hbm, a, b, x, y, sem_in, sem_out):
+    parts = [
+        (arrays, pl.ds(32 * half, 32), 2 * half + n)
+        for half in range(2)
+        for n, arrays in enumerate(((a_hbm, a, x, x_hbm), (b_hbm, b, y, y_hbm)))
+    ]
+    ins = [pltpu.make_async_copy(r[0].at[p], r[1].at[p], sem_in.at[k]) for r, p, k in parts]
+    outs = [pltpu.make_async_copy(r[2].at[p], r[3].at[p], sem_out.at[k]) for r, p, k in parts]
+    for c in ins:
+        c.start()
+    for c, out, (r, p, _) in zip(ins, outs, parts):
+        c.wait()
+        r[2][p] = r[1][p]
+        out.start()
+    for out in outs:
+        out.wait()
 
 
 def on_device(volume, cotangent, gain_width, qkv_width, out_width, gain_height, qkv_height, out_height):
     shape = volume.shape
-    vm = pl.BlockSpec(memory_space=pltpu.VMEM)
     hbm = pl.BlockSpec(memory_space=pl.ANY)
     flat = jax.ShapeDtypeStruct((64, 4, D), BF)
     v = lambda *s: pltpu.VMEM(s, BF)
     result, grad = pl.pallas_call(
         kernel,
         out_shape=(flat, flat),
-        in_specs=[vm, vm, vm, vm, hbm, hbm, hbm, hbm],
-        out_specs=(vm, vm),
+        in_specs=[hbm] * 8,
+        out_specs=(hbm, hbm),
         scratch_shapes=[
-            v(D, 3 * INNER), v(INNER, D), v(D, 3 * INNER), v(INNER, D), v(3, TOK, TOK), v(2, 128, 128),
+            v(64, 4, D), v(64, 4, D), v(64, 4, D), v(64, 4, D), v(D), v(D), v(D, 3 * INNER), v(INNER, D), v(D, 3 * INNER), v(INNER, D), v(4, TOK, TOK), v(128, 128),
             v(2, 32, 8, 512), v(2, 32, 8, 512), v(2, 64, 8, 128), v(2, 64, 8, 128),
-            v(2, 64, 8, 128), v(2, 64, 8, 128), v(2, 32, 8, 512), v(2, 32, 8, 512),
+            v(64, 16, 128), v(64, 16, 128), v(2, 32, 8, 512), v(2, 32, 8, 512),
             v(16, 2, 8, D), v(2, 2, 8, 8, D), v(16, 2, 8, D), v(2, 2, 8, 8, D),
             v(2, 2, 8, 8, D), v(16, 2, 8, D), v(2, 2, 8, 8, D), v(16, 2, 8, D),
             v(TOK, 3 * INNER), v(TOK, 3 * INNER), pltpu.VMEM((8, TOK, 128), F32), pltpu.VMEM((8, TOK, 128), F32),
             v(TOK, INNER), v(TOK, INNER), v(TOK, 3 * INNER), v(TOK, INNER), v(TOK, INNER), v(TOK, D),
-            pltpu.SemaphoreType.DMA((4,)), pltpu.SemaphoreType.DMA((12,)), pltpu.SemaphoreType.DMA((12,)),
+            pltpu.SemaphoreType.DMA((8,)), pltpu.SemaphoreType.DMA((2,)), pltpu.SemaphoreType.DMA((12,)), pltpu.SemaphoreType.DMA((12,)),
             pltpu.SemaphoreType.DMA,
         ],
         compiler_params=pltpu.CompilerParams(
@@ -421,7 +458,13 @@
         volume.reshape(64, 4, D), cotangent.reshape(64, 4, D), gain_width, gain_height,
         qkv_width, out_width, qkv_height, out_height,
     )
-    result, grad = pl.pallas_call(hand_over, out_shape=(flat, flat), in_specs=[vm, vm], out_specs=(vm, vm))(result, grad)
+    result, grad = pl.pallas_call(
+        hand_over,
+        out_shape=(flat, flat),
+        in_specs=[hbm, hbm],
+        out_specs=(hbm, hbm),
+        scratch_shapes=[v(64, 4, D)] * 4 + [pltpu.SemaphoreType.DMA((4,))] * 2,
+    )(result, grad)
     return result.reshape(shape), grad.reshape(shape)
 
 

time: 74.5 us -> 72.2 us (0.969)
  Pallas kernels: 73.7 us -> 71.3 us
    pallas_call x2, Pallas kernels: 73.7 us -> 71.3 us  [the longest x1 69.3 us: on_device(): pl.pallas_call(kernel, out_shape=(flat, flat), in_specs=[hbm] * 8, out_sp...]
where the time goes in v3:
time: 72.2 us; the launch traced here: 72.1 us
  Pallas kernels  71.3 us (99%)
  between operations  0.8 us (1%)
    pallas_call x1, Pallas kernels, on_device(): pl.pallas_call(kernel, out_shape=(flat, flat), in_specs=[hbm] * 8, out_sp...  69.3 us
    pallas_call x1, Pallas kernels, on_device(): pl.pallas_call(hand_over, out_shape=(flat, flat), in_specs=[hbm, hbm], ou...  2 us

profile of v3, /device:TPU:1, one launch (start us, length us, event | category | flops | bytes accessed | tf_op | source)
XLA Modules:
  0.0 72.1 jit_solution(9765817461524473603)
XLA Ops:
  0.6 69.3 %shard_map.95 = (bf16[64,4,1024]{2,1,0:T(4,128)(2,1)}, bf16[64,4,1024]{2,1,0:T(4,128)(2,1)}) custom-call(bf16[64,4,1024]{2,1,0:T(4,128)(2,1)} %bitcast.4, bf16[64,4,1024]{2,1,0:T(4,128)(2,1)} %bitcast.5, bf16[1024]{0:T(1024)(128)(2,1)} %gw_hbm.1, bf16[1024]{0:T(1024)(128)(2,1)} %gh_hbm.1, bf16[1024,1536]{1,0:T(8,128)(2,1)} %qkvw_hbm.1, ...), custom_call_target="tpu_custom_call" | custom-call | tf_op jit(solution)/shard_map/pallas_call | solution.py:438
  70.0 2.0 %shard_map.96 = (bf16[64,4,1024]{2,1,0:T(4,128)(2,1)}, bf16[64,4,1024]{2,1,0:T(4,128)(2,1)}) custom-call(bf16[64,4,1024]{2,1,0:T(4,128)(2,1)} %get-tuple-element.6.a_hbm, bf16[64,4,1024]{2,1,0:T(4,128)(2,1)} %get-tuple-element.7.b_hbm), custom_call_target="tpu_custom_call" | custom-call | tf_op jit(solution)/shard_map/pallas_call | solution.py:461

commit v4 on v3

--- a/solution.py
+++ b/solution.py
@@ -334,14 +334,14 @@
     loads[2].wait()
     loads[3].wait()
 
+    wait_inner(r1, 0, recv_sem.at[0])
+    wait_inner(r1, 1, recv_sem.at[1])
+    got = r1[...].astype(F32).reshape(32, 2, 8, D // 2)
+    tokens = unpack_tokens(got[:, 0], got[:, 1]).astype(BF)
+    proj[...] = dot(tokens, qkvw[...]).astype(BF)
     for line in range(2):
-        rows = pl.ds(line * 128, 128)
-        wait_inner(r1, line, recv_sem.at[line])
-        got = r1[line].astype(F32).reshape(16, 2, 8, D // 2)
-        tokens = unpack_tokens(got[:, 0], got[:, 1]).astype(BF)
-        proj[rows] = dot(tokens, qkvw[...]).astype(BF)
         attend(proj, probs, mixed, line)
-        s2[line] = pack_pairs(mixed[rows].astype(F32))
+        s2[line] = pack_pairs(mixed[pl.ds(line * 128, 128)].astype(F32))
         width_to_height(line)
 
     loads[4].wait()

time: 72.2 us -> 72.7 us (level)
  no operation moved by 1% of the time
where the time goes in v4:
time: 72.7 us; the launch traced here: 72.6 us
  Pallas kernels  71.8 us (99%)
  between operations  0.8 us (1%)
    pallas_call x1, Pallas kernels, on_device(): pl.pallas_call(kernel, out_shape=(flat, flat), in_specs=[hbm] * 8, out_sp...  69.8 us
    pallas_call x1, Pallas kernels, on_device(): pl.pallas_call(hand_over, out_shape=(flat, flat), in_specs=[hbm, hbm], ou...  2 us

profile of v4, /device:TPU:1, one launch (start us, length us, event | category | flops | bytes accessed | tf_op | source)
XLA Modules:
  0.0 72.6 jit_solution(2502609352263198706)
XLA Ops:
  0.6 69.8 %shard_map.95 = (bf16[64,4,1024]{2,1,0:T(4,128)(2,1)}, bf16[64,4,1024]{2,1,0:T(4,128)(2,1)}) custom-call(bf16[64,4,1024]{2,1,0:T(4,128)(2,1)} %bitcast.4, bf16[64,4,1024]{2,1,0:T(4,128)(2,1)} %bitcast.5, bf16[1024]{0:T(1024)(128)(2,1)} %gw_hbm.1, bf16[1024]{0:T(1024)(128)(2,1)} %gh_hbm.1, bf16[1024,1536]{1,0:T(8,128)(2,1)} %qkvw_hbm.1, ...), custom_call_target="tpu_custom_call" | custom-call | tf_op jit(solution)/shard_map/pallas_call | solution.py:438
  70.5 2.0 %shard_map.96 = (bf16[64,4,1024]{2,1,0:T(4,128)(2,1)}, bf16[64,4,1024]{2,1,0:T(4,128)(2,1)}) custom-call(bf16[64,4,1024]{2,1,0:T(4,128)(2,1)} %get-tuple-element.6.a_hbm, bf16[64,4,1024]{2,1,0:T(4,128)(2,1)} %get-tuple-element.7.b_hbm), custom_call_target="tpu_custom_call" | custom-call | tf_op jit(solution)/shard_map/pallas_call | solution.py:461
